TPU v7x, 32 devices: a whole 2x2x4 slice. The times are simulated.
32 devices in a mesh: batch: 2 (over x), head: 2 (over y), blk: 8 (over z, core).
Axes of the slice: x: 2, y: 2, z: 4, core: 2. Of those that a mesh axis runs over, the one named last changes fastest.
Arguments:
- tokens: bfloat16 [16, 2048, 1024], P(('batch', 'blk'), 'head'), parts along dimension 0, may hold values from -10.5 to 10.5
- proj_weight: bfloat16 [1024, 3072], replicated, may hold values from -0.1875 to 0.1875
- out_weight: bfloat16 [1024, 1024], replicated, may hold values from -1.5 to 1.5
- pattern: int32 [256, 16], P(('batch', 'blk')), parts along dimension 0, may hold values from 0 to 127, as said below
Outputs:
- mixed_out: bfloat16 [16, 2048, 1024], P(('batch', 'blk'), 'head'), parts along dimension 0
There are 2 independent parts, one for each index of `batch`. A program takes and returns all parts, laid end to end along the dimension named above; an argument that names none is the same for every part. Nothing has to cross between parts.
Inputs may be any that keep to these rules, and one draw needn't show every extreme that they name: `pattern`: row i lists first 6 distinct blocks j with |j - i| <= 8, among them i itself, then 10 distinct summary blocks j (j % 16 >= 12) with |j - i| > 8. Every row with 8 <= i < 120 lists i - 8 and i + 8.
All inputs are finite; a program needn't handle non-finite values.
Results may differ from a plain program's by a relative error of at most 0.0095.
Values may be sent and summed in bfloat16 or wider, within the bound.
No kernel may reach another device: no remote copies, remote signals or barrier semaphores. Data moves between devices by JAX's collectives and lax.ppermute only.
A program may use at most 128 MiB of HBM per device.

v0:
```python
import functools

import jax
import jax.numpy as jnp
from jax import lax
from jax.experimental import pallas as pl
from jax.experimental.pallas import tpu as pltpu
from jax.sharding import PartitionSpec as P

D = 1024
H = 16
HD = 64
BLK = 128
REACH = 8
LSEL = 6
SUMB = 4
SB = 16
KSEL = 16
PAIRS = H // 2
LANES = 2 * HD
TOTAL_CAP = 2.0**100


def split_kernel(weight_ref, query_ref, key_ref, value_ref):
    both = weight_ref[...]
    first, second = both[:, : 3 * HD], both[:, 3 * HD :]

    def columns(which):
        lo = which * HD
        return jnp.concatenate([first[:, lo : lo + HD], second[:, lo : lo + HD]], axis=1)

    query_ref[...] = columns(0).T
    key_ref[...] = columns(1)
    value_ref[...] = columns(2).T


def split_weights(proj_weight):
    wide = jax.ShapeDtypeStruct((D, D), jnp.bfloat16)
    across = pl.BlockSpec((LANES, D), lambda p: (p, 0))
    down = pl.BlockSpec((D, LANES), lambda p: (0, p))
    return pl.pallas_call(
        split_kernel,
        grid=(PAIRS,),
        in_specs=[pl.BlockSpec((D, 3 * LANES), lambda p: (0, p))],
        out_specs=[across, down, across],
        out_shape=[wide, wide, wide],
        cost_estimate=pl.CostEstimate(flops=0, bytes_accessed=4 * D * 3 * D, transcendentals=0),
        name="split_weights",
    )(proj_weight)


def attend_kernel(first, last, blocks, count, together, chunk, pieces, *refs):
    f32, bf16 = jnp.float32, jnp.bfloat16
    refs = list(refs)
    table_ref, query_ref = refs[:2]
    key_refs = refs[2 : 2 + pieces]
    value_refs = refs[2 + pieces : 2 + 2 * pieces]
    refs = refs[2 + 2 * pieces :]
    if not first:
        sum_in_ref, row_in_ref = refs[:2]
        refs = refs[2:]
    if last:
        out_ref = refs.pop(0)
    else:
        sum_out_ref, row_out_ref = refs[:2]
        refs = refs[2:]
    if first:
        shift_ref = refs.pop()
    if pieces == 1:
        key_ref, value_ref = key_refs[0], value_refs[0]
    else:
        key_ref, value_ref = refs
        start = 0
        for key_piece, value_piece in zip(key_refs, value_refs):
            size = key_piece.shape[0]
            key_ref[start : start + size, :] = key_piece[...]
            value_ref[:, start : start + size] = value_piece[...]
            start += size

    row = lax.broadcasted_iota(jnp.int32, (LANES, BLK), 0)

    def at(index, size=BLK):
        return pl.ds(pl.multiple_of(index * size, size), size)

    def queries(index):
        own = query_ref[:, at(index)]
        zero = jnp.zeros_like(own)
        return jnp.concatenate([jnp.where(row < HD, own, zero), jnp.where(row < HD, zero, own)], axis=1)

    def places(index, which, size):
        return [pl.multiple_of(table_ref[index, which + n] * BLK, BLK) for n in range(size)]

    def score(index, which, size, query):
        keys = [key_ref[pl.ds(place, BLK), :] for place in places(index, which, size)]
        return jnp.dot(jnp.concatenate(keys, axis=0), query, preferred_element_type=f32)

    def values(index, which, size):
        return jnp.concatenate([value_ref[:, pl.ds(place, BLK)] for place in places(index, which, size)], axis=1)

    def gather(picked, raised):
        ones = jnp.ones((16, raised.shape[0]), bf16)
        return jnp.dot(jnp.concatenate([picked, ones], axis=0), raised, preferred_element_type=f32)

    def by_head(rows):
        return jnp.where(row < HD, rows[:, :BLK], rows[:, BLK:])

    def finish(index, shift, total, rescale=None):
        mine = jnp.concatenate([total[:HD, :BLK], total[HD:LANES, BLK:]], axis=0)
        count_all = total[LANES : LANES + 1]
        if not first:
            before = sum_in_ref[:, at(index)]
            count_before = row_in_ref[0, 1:2, at(index, 2 * BLK)]
            if rescale is not None:
                before = before * by_head(rescale)
                count_before = count_before * rescale
            mine = mine + before
            count_all = count_all + count_before
        if last:
            out_ref[at(index), :] = (mine * by_head(1.0 / count_all)).T.astype(bf16)
        else:
            sum_out_ref[:, at(index)] = mine
            row_out_ref[0, 0:1, at(index, 2 * BLK)] = shift
            row_out_ref[0, 1:2, at(index, 2 * BLK)] = count_all
        return count_all

    def whole_row(index):
        query = queries(index)
        shift = jnp.full((1, 2 * BLK), -jnp.inf, f32) if first else row_in_ref[0, 0:1, at(index, 2 * BLK)]
        old = shift

        def largest(n, shift):
            return jnp.maximum(shift, jnp.max(score(index, 2 * n, 2, query), axis=0, keepdims=True))

        shift = lax.fori_loop(0, count // 2, largest, shift)

        def add(n, total):
            raised = jnp.exp(score(index, 2 * n, 2, query) - shift).astype(bf16)
            return total + gather(values(index, 2 * n, 2), raised)

        total = lax.fori_loop(0, count // 2, add, jnp.zeros((LANES + 16, 2 * BLK), f32))
        finish(index, shift, total, None if first else jnp.exp(old - shift))

    def one(index):
        query = queries(index)
        total = None
        shift = shift_ref[pl.ds(index, 1), :] if first else row_in_ref[0, 0:1, at(index, 2 * BLK)]
        for which in range(0, count, chunk):
            size = min(chunk, count - which)
            scores = score(index, which, size, query)
            part = gather(values(index, which, size), jnp.exp(scores - shift).astype(bf16))
            total = part if total is None else total + part
        return finish(index, shift, total)

    if first:
        for index in range(blocks):
            shift_ref[index : index + 1, :] = jnp.max(score(index, 0, 1, queries(index)), axis=0, keepdims=True)

    def body(number, peak):
        for n in range(together):
            peak = jnp.maximum(peak, one(number * together + n))
        return peak

    peak = lax.fori_loop(0, blocks // together, body, jnp.zeros((1, 2 * BLK), f32))

    @pl.when(jnp.logical_not(jnp.max(peak) <= TOTAL_CAP))
    def _():
        lax.fori_loop(0, blocks, lambda index, carry: (whole_row(index), carry)[1], 0)


def attend(name, table, query, keys, values, state, last, together, chunk):
    f32, bf16 = jnp.float32, jnp.bfloat16
    rows = query.shape[1]
    blocks = rows // BLK
    count = table.shape[1]
    while blocks % together:
        together //= 2
    total_rows = sum(key.shape[0] for key in keys)
    across = lambda array: pl.BlockSpec((LANES, array.shape[1]), lambda p: (p, 0))
    down = lambda array: pl.BlockSpec((array.shape[0], LANES), lambda p: (0, p))
    per_row = pl.BlockSpec((1, 2, 2 * rows), lambda p: (p, 0, 0))
    in_specs = [pl.BlockSpec(memory_space=pltpu.SMEM), across(query)]
    in_specs += [down(key) for key in keys] + [across(value) for value in values]
    if state:
        in_specs += [across(query), per_row]
    if last:
        out_specs = pl.BlockSpec((rows, LANES), lambda p: (0, p))
        out_shape = jax.ShapeDtypeStruct((rows, D), bf16)
    else:
        out_specs = [across(query), per_row]
        out_shape = [jax.ShapeDtypeStruct((D, rows), f32), jax.ShapeDtypeStruct((PAIRS, 2, 2 * rows), f32)]
    scratch = [pltpu.VMEM((total_rows, LANES), bf16), pltpu.VMEM((LANES, total_rows), bf16)]
    scratch = scratch if len(keys) > 1 else []
    if not state:
        scratch.append(pltpu.VMEM((blocks, 2 * BLK), f32))
    scores = rows * count * BLK * H
    return pl.pallas_call(
        functools.partial(attend_kernel, not state, last, blocks, count, together, chunk, len(keys)),
        grid=(PAIRS,),
        in_specs=in_specs,
        out_specs=out_specs,
        out_shape=out_shape,
        scratch_shapes=scratch,
        compiler_params=pltpu.CompilerParams(vmem_limit_bytes=18 * 2**20),
        cost_estimate=pl.CostEstimate(
            flops=24 * scores * HD, bytes_accessed=4 * total_rows * D + 10 * rows * D, transcendentals=scores
        ),
        name=name,
    )(table, query, *keys, *values, *state)


def project_rows(rows, weight):
    return jnp.dot(rows, weight, preferred_element_type=jnp.float32).astype(jnp.bfloat16)


def project_columns(weight, rows, scale=1.0):
    wide = lax.dot_general(weight, rows, (((1,), (1,)), ((), ())), preferred_element_type=jnp.float32)
    return (wide * scale).astype(jnp.bfloat16)


def rows_by_axes(own, weights, place, stride, strides):
    summary = SUMB * BLK
    half = summary // 2
    cut = own.shape[0] - summary
    chips = strides // 2
    low = place == 0
    swap = lambda rows: lax.ppermute(rows, "head", [(0, 1), (1, 0)])
    beside = lambda rows: lax.ppermute(rows, "blk", [(s, s ^ 1) for s in range(strides)])

    def along(rows, k):
        return lax.ppermute(rows, "blk", [(s, (s + 2 * k) % strides) for s in range(strides)])

    steps = []
    for s in range(strides - 1):
        steps += [(s, s + 1), (strides + s + 1, strides + s)]
    to_next = lambda rows: lax.ppermute(rows, ("head", "blk"), steps)

    other_end = swap(own[-half:])
    other_end, own, weights = lax.optimization_barrier((other_end, own, weights))
    carried = jnp.where(low, other_end, own[cut : cut + half])
    other = swap(own[:-half])
    slots = [along(carried, k) for k in range(1, chips)]
    edge_end = to_next(other_end)
    own, other, other_end = lax.optimization_barrier((own, other, other_end))
    query = project_columns(weights[0], own, HD**-0.5)
    query, *slots = lax.optimization_barrier((query, *slots))
    across = [swap(rows) for rows in slots]
    foreign = jnp.concatenate(slots, axis=0)
    nearby = jnp.where(low, jnp.concatenate([other_end, other[-half:]], axis=0), own[cut:])
    near_rows = [own, other, other_end, to_next(other), edge_end]
    far_rows = [nearby, beside(nearby), foreign, beside(foreign)]
    span = 2 * (chips - 1)

    def late_rows(state):
        state, arrived = lax.optimization_barrier((state, across))
        arrived = jnp.concatenate(arrived, axis=0)
        return state, [arrived, beside(arrived)]

    def position(block):
        of, inside = block // SB, block % SB
        rel = block - stride * SB
        mine = inside % 8 + jnp.where(inside // 8 == place, 0, 8)
        edge = jnp.where(rel < 0, rel + SB + 8, rel)
        order = inside - (SB - SUMB)
        k = (stride // 2 - of // 2) % chips
        turned = (order // 2 ^ (1 - place)) * 2 + order % 2
        beside_me = jnp.where(of % 2 == stride % 2, 0, 1)
        part = beside_me + jnp.where(order // 2 == 1 - place, 0, 2)
        far = jnp.where(k == 0, 4 * beside_me + turned, 8 + part * span + (k - 1) * 2 + order % 2)
        return jnp.where(of == stride, mine, edge), far

    return near_rows, far_rows, late_rows, weights, query, position


def rows_by_gather(own, place, stride, strides, heads):
    summary = SUMB * BLK
    share = summary // heads
    lower = place < heads // 2
    stride_rows = lax.all_gather(own, "head", axis=0, tiled=True)
    piece = lax.dynamic_slice_in_dim(stride_rows[-summary:], place * share, share, 0)
    far_rows = lax.all_gather(piece, ("blk", "head"), axis=0, tiled=True)
    half = stride_rows.shape[0] // 2
    steps = []
    for h in range(heads):
        for s in range(strides - 1):
            ends = (h * strides + s, h * strides + s + 1)
            steps.append(ends if h < heads // 2 else ends[::-1])
    edge = lax.ppermute(jnp.where(lower, stride_rows[half:], stride_rows[:half]), ("head", "blk"), steps)

    def position(block):
        rel = block - stride * SB
        near = jnp.where(rel < 0, rel + SB + REACH, rel)
        return near, block // SB * SUMB + block % SB - (SB - SUMB)

    return [stride_rows, edge], [far_rows], lambda state: (state, []), position


def on_device(tokens, proj_weight, out_weight, pattern):
    heads = lax.axis_size("head")
    strides = lax.axis_size("blk")
    place = lax.axis_index("head")
    stride = lax.axis_index("blk")
    own = tokens[0]
    blocks = own.shape[0] // BLK
    weights = split_weights(proj_weight)

    if heads == 2:
        near_rows, far_rows, late_rows, weights, query, position = rows_by_axes(
            own, weights, place, stride, strides
        )
    else:
        near_rows, far_rows, late_rows, position = rows_by_gather(own, place, stride, strides, heads)
        query = project_columns(weights[0], own, HD**-0.5)
    listed = lax.dynamic_slice_in_dim(pattern, place * blocks, blocks, 0)
    near = position(listed[:, :LSEL])[0]
    far = position(listed[:, LSEL:])[1]

    _, key_weight, value_weight = weights
    both = lambda pieces: (
        [project_rows(rows, key_weight) for rows in pieces],
        [project_columns(value_weight, rows) for rows in pieces],
    )
    near_keys, near_values = both(near_rows)
    far_keys, far_values = both(far_rows)
    state = attend("attend_near", near, query, near_keys, near_values, [], False, 2, 4)
    state, late = late_rows(state)
    late_keys, late_values = both(late)
    mixed = attend("attend_far", far, query, far_keys + late_keys, far_values + late_values, state, True, 2, 4)
    out = jnp.dot(mixed, out_weight, preferred_element_type=jnp.float32).astype(jnp.bfloat16)
    return out.reshape(tokens.shape)


def solution(mesh):
    return jax.shard_map(
        on_device,
        mesh=mesh,
        in_specs=(P(("batch", "blk"), "head", None), P(), P(), P(("batch", "blk"), None)),
        out_specs=P(("batch", "blk"), "head", None),
        check_vma=False,
    )
```

profile of v0, /device:TPU:11, one launch (start us, length us, event | category | flops | bytes accessed | tf_op | source)
XLA Modules:
  0.0 295.2 jit_solution(9716787446703695830)
XLA Ops:
  1.2 1.3 collective-permute-start
  2.5 8.6 %split_weights.1 = (bf16[1024,1024]{1,0:T(8,128)(2,1)}, bf16[1024,1024]{1,0:T(8,128)(2,1)}, bf16[1024,1024]{1,0:T(8,128)(2,1)}) custom-call(bf16[1024,3072]{1,0:T(8,128)(2,1)} %weight_ref.1), custom_call_target="tpu_custom_call" | custom-call | bytes 12582912 | tf_op jit(solution)/shard_map/split_weights/pallas_call | solution.py:41
  11.2 2.9 collective-permute-done
  14.1 2.7 slice.27
  18.0 4.9 %collective-permute-start.8 = (bf16[256,1024]{1,0:T(8,128)(2,1)S(1)}, bf16[256,1024]{1,0:T(8,128)(2,1)S(1)}, u32[]{:S(2)}, u32[]{:S(2)}) collective-permute-start(bf16[256,1024]{1,0:T(8,128)(2,1)S(1)} %collective-permute-done), channel_id=1, source_target_pairs={{0,1},{9,8},{1,2},{10,9},{2,3},{11,10},{3,4},{12,11},{4,5},{13,12}... | collective-permute-start | bytes 1572872 | tf_op jit(solution)/shard_map/ppermute | solution.py:235
  24.2 1.3 collective-permute-start.2
  26.8 5.8 %collective-permute-done.8 = bf16[256,1024]{1,0:T(8,128)(2,1)S(1)} collective-permute-done((bf16[256,1024]{1,0:T(8,128)(2,1)S(1)}, bf16[256,1024]{1,0:T(8,128)(2,1)S(1)}, u32[]{:S(2)}, u32[]{:S(2)}) %collective-permute-start.8) | collective-permute-done | bytes 524320 | tf_op jit(solution)/shard_map/ppermute | solution.py:235
  32.7 2.3 convolution_convert_fusion.18.refs_11_
  35.8 15.7 %collective-permute-done.1 = bf16[768,1024]{1,0:T(8,128)(2,1)} collective-permute-done((bf16[768,1024]{1,0:T(8,128)(2,1)}, bf16[768,1024]{1,0:T(8,128)(2,1)}, u32[]{:S(2)}, u32[]{:S(2)}) %collective-permute-start.1) | collective-permute-done | bytes 1572896 | tf_op jit(solution)/shard_map/ppermute | solution.py:226
  51.5 5.7 %collective-permute-start.7 = (bf16[768,1024]{1,0:T(8,128)(2,1)}, bf16[768,1024]{1,0:T(8,128)(2,1)S(1)}, u32[]{:S(2)}, u32[]{:S(2)}) collective-permute-start(bf16[768,1024]{1,0:T(8,128)(2,1)} %collective-permute-done.1), channel_id=1, source_target_pairs={{0,1},{9,8},{1,2},{10,9},{2,3},{11,10},{3,4},{12,11},{4,5},{13,12}... | collective-permute-start | bytes 4718600 | tf_op jit(solution)/shard_map/ppermute | solution.py:235
  57.2 3.2 %convolution_convert_fusion.11.refs_3_ = bf16[768,1024]{1,0:T(8,128)(2,1)S(1)} fusion(bf16[768,1024]{1,0:T(8,128)(2,1)} %collective-permute-done.1, bf16[1024,1024]{1,0:T(8,128)(2,1)S(1)} %copy-done.3), kind=kOutput, calls=%fused_computation.13 | convolution fusion | flops 1611399168 | bytes 5242880 | tf_op jit(solution)/shard_map/dot_general | solution.py:212
  60.4 3.4 %convolution_convert_fusion.9.refs_8_ = bf16[1024,768]{1,0:T(8,128)(2,1)S(1)} fusion(bf16[1024,1024]{1,0:T(8,128)(2,1)S(1)} %copy-done.4, bf16[768,1024]{1,0:T(8,128)(2,1)} %collective-permute-done.1), kind=kOutput, calls=%fused_computation.11 | convolution fusion | flops 1611399168 | bytes 5242880 | tf_op jit(solution)/shard_map/dot_general | solution.py:216
  63.9 2.4 convolution_convert_fusion.refs_7_
  66.3 2.4 multiply_convert_fusion.refs_1_
  68.7 5.4 %collective-permute-done.3 = bf16[256,1024]{1,0:T(8,128)(2,1)S(1)} collective-permute-done((bf16[256,1024]{1,0:T(8,128)(2,1)S(1)}, bf16[256,1024]{1,0:T(8,128)(2,1)S(1)}, u32[]{:S(2)}, u32[]{:S(2)}) %collective-permute-start.3) | collective-permute-done | bytes 524320 | tf_op jit(solution)/shard_map/ppermute | solution.py:230
  75.2 1.5 collective-permute-start.10
  76.9 1.8 convolution_convert_fusion.5.refs_10_
  78.7 1.8 convolution_convert_fusion.13.refs_4_
  80.9 2.5 collective-permute-start.5
  84.7 1.5 convolution_convert_fusion.17.refs_2_
  87.7 2.3 convolution_convert_fusion.1.refs_2_
  92.7 1.8 convolution_convert_fusion.10.refs_5_
  94.5 1.8 convolution_convert_fusion.8.refs_10_
  96.4 138.6 %attend_near.1 = (f32[1024,1024]{1,0:T(8,128)S(1)}, f32[8,2,2048]{2,1,0:T(2,128)S(1)}) custom-call(s32[8,6]{1,0:T(8,128)S(1)} %fusion.12.refs_0_, bf16[1024,1024]{1,0:T(8,128)(2,1)S(1)} %multiply_convert_fusion.refs_1_, bf16[1024,1024]{1,0:T(8,128)(2,1)S(1)} %convolution_convert_fusion.1.refs_2_, bf16[768,1024]{1,0:T(8,128)(2,1)S(1)} %convolution_convert_fusion.11.refs_3_, ...), custom_call_target="tpu_custom_call" | custom-call | flops 19327352832 | bytes 23068672 | tf_op jit(solution)/shard_map/attend_near/pallas_call | solution.py:196
  235.7 1.8 convolution_convert_fusion.3.refs_12_
  237.6 1.8 convolution_convert_fusion.7.refs_6_
  239.4 1.8 convolution_convert_fusion.4.refs_11_
  241.2 1.8 convolution_convert_fusion.12.refs_5_
  243.0 1.8 convolution_convert_fusion.2.refs_13_
  244.9 1.8 convolution_convert_fusion.6.refs_7_
  246.7 44.8 %attend_far.1 = bf16[1024,1024]{1,0:T(8,128)(2,1)S(1)} custom-call(s32[8,10]{1,0:T(8,128)S(1)} %fusion.1.refs_0_, bf16[1024,1024]{1,0:T(8,128)(2,1)S(1)} %multiply_convert_fusion.refs_1_, bf16[512,1024]{1,0:T(8,128)(2,1)S(1)} %convolution_convert_fusion.17.refs_2_, bf16[512,1024]{1,0:T(8,128)(2,1)S(1)} %convolution_convert_fusion.16.refs_3_, ...), custom_call_target="tpu_custom_call" | custom-call | flops 32212254720 | bytes 27262976 | tf_op jit(solution)/shard_map/attend_far/pallas_call | solution.py:196
  291.5 3.7 %convert_bitcast_fusion = bf16[1,1024,1024]{2,1,0:T(8,128)(2,1)} fusion(bf16[1024,1024]{1,0:T(8,128)(2,1)S(1)} %attend_far.1, bf16[1024,1024]{1,0:T(8,128)(2,1)S(1)} %copy-done), kind=kOutput, calls=%fused_computation.1 | convolution fusion | flops 2148532224 | bytes 6291456 | tf_op jit(solution)/shard_map/dot_general | solution.py:328
  (47 shorter events, 13.5 us)
Async XLA Ops:
  0.0 291.5 %copy-start = (bf16[1024,1024]{1,0:T(8,128)(2,1)S(1)}, bf16[1024,1024]{1,0:T(8,128)(2,1)}, u32[]{:S(2)}) copy-start(bf16[1024,1024]{1,0:T(8,128)(2,1)} %param.6) | copy-start | bytes 6291460
  1.2 12.9 %collective-permute-start = (bf16[256,1024]{1,0:T(8,128)(2,1)S(1)}, bf16[256,1024]{1,0:T(8,128)(2,1)S(1)}, u32[]{:S(2)}, u32[]{:S(2)}) collective-permute-start(bf16[256,1024]{1,0:T(8,128)(2,1)S(1)} %slice_bitcast_fusion), channel_id=1, source_target_pairs={{0,8},{8,0},{1,9},{9,1},{2,10},{10,2},{3,11},{11,3},{4,12},{12,4},... | collective-permute-start | bytes 1572872 | tf_op jit(solution)/shard_map/ppermute | solution.py:226
  11.1 6.9 %copy-start.2 = (s32[16,16]{1,0:T(8,128)S(1)}, s32[16,16]{1,0:T(8,128)}, u32[]{:S(2)}) copy-start(s32[16,16]{1,0:T(8,128)} %param.7) | copy-start | bytes 3076
  16.8 34.7 %collective-permute-start.1 = (bf16[768,1024]{1,0:T(8,128)(2,1)}, bf16[768,1024]{1,0:T(8,128)(2,1)}, u32[]{:S(2)}, u32[]{:S(2)}) collective-permute-start(bf16[768,1024]{1,0:T(8,128)(2,1)} %slice.27), channel_id=1, source_target_pairs={{0,8},{8,0},{1,9},{9,1},{2,10},{10,2},{3,11},{11,3},{4,12},{12,4},... | collective-permute-start | bytes 4718600 | tf_op jit(solution)/shard_map/ppermute | solution.py:226
  18.0 14.6 %collective-permute-start.8 = (bf16[256,1024]{1,0:T(8,128)(2,1)S(1)}, bf16[256,1024]{1,0:T(8,128)(2,1)S(1)}, u32[]{:S(2)}, u32[]{:S(2)}) collective-permute-start(bf16[256,1024]{1,0:T(8,128)(2,1)S(1)} %collective-permute-done), channel_id=1, source_target_pairs={{0,1},{9,8},{1,2},{10,9},{2,3},{11,10},{3,4},{12,11},{4,5},{13,12}... | collective-permute-start | bytes 1572872 | tf_op jit(solution)/shard_map/ppermute | solution.py:235
  24.2 10.8 %copy-start.3 = (bf16[1024,1024]{1,0:T(8,128)(2,1)S(1)}, bf16[1024,1024]{1,0:T(8,128)(2,1)}, u32[]{:S(2)}) copy-start(bf16[1024,1024]{1,0:T(8,128)(2,1)} %get-tuple-element.37) | copy-start | bytes 6291460
  24.2 44.4 %collective-permute-start.2 = (bf16[256,1024]{1,0:T(8,128)(2,1)S(1)}, bf16[256,1024]{1,0:T(8,128)(2,1)S(1)}, u32[]{:S(2)}, u32[]{:S(2)}) collective-permute-start(bf16[256,1024]{1,0:T(8,128)(2,1)S(1)} %slice_select_fusion), channel_id=1, source_target_pairs={{0,2},{1,3},{2,4},{3,5},{4,6},{5,7},{6,0},{7,1},{8,10},{9,11},{10,... | collective-permute-start | bytes 1572872 | tf_op jit(solution)/shard_map/ppermute | solution.py:230
  25.6 48.5 %collective-permute-start.3 = (bf16[256,1024]{1,0:T(8,128)(2,1)S(1)}, bf16[256,1024]{1,0:T(8,128)(2,1)S(1)}, u32[]{:S(2)}, u32[]{:S(2)}) collective-permute-start(bf16[256,1024]{1,0:T(8,128)(2,1)S(1)} %slice_select_fusion), channel_id=1, source_target_pairs={{0,4},{1,5},{2,6},{3,7},{4,0},{5,1},{6,2},{7,3},{8,12},{9,13},{10,... | collective-permute-start | bytes 1572872 | tf_op jit(solution)/shard_map/ppermute | solution.py:230
  26.5 47.5 %collective-permute-start.4 = (bf16[256,1024]{1,0:T(8,128)(2,1)S(1)}, bf16[256,1024]{1,0:T(8,128)(2,1)S(1)}, u32[]{:S(2)}, u32[]{:S(2)}) collective-permute-start(bf16[256,1024]{1,0:T(8,128)(2,1)S(1)} %slice_select_fusion), channel_id=1, source_target_pairs={{0,6},{1,7},{2,0},{3,1},{4,2},{5,3},{6,4},{7,5},{8,14},{9,15},{10,... | collective-permute-start | bytes 1572872 | tf_op jit(solution)/shard_map/ppermute | solution.py:230
  35.8 24.6 %copy-start.4 = (bf16[1024,1024]{1,0:T(8,128)(2,1)S(1)}, bf16[1024,1024]{1,0:T(8,128)(2,1)}, u32[]{:S(2)}) copy-start(bf16[1024,1024]{1,0:T(8,128)(2,1)} %get-tuple-element.41) | copy-start | bytes 6291460
  51.5 41.2 %collective-permute-start.7 = (bf16[768,1024]{1,0:T(8,128)(2,1)}, bf16[768,1024]{1,0:T(8,128)(2,1)S(1)}, u32[]{:S(2)}, u32[]{:S(2)}) collective-permute-start(bf16[768,1024]{1,0:T(8,128)(2,1)} %collective-permute-done.1), channel_id=1, source_target_pairs={{0,1},{9,8},{1,2},{10,9},{2,3},{11,10},{3,4},{12,11},{4,5},{13,12}... | collective-permute-start | bytes 4718600 | tf_op jit(solution)/shard_map/ppermute | solution.py:235
  60.4 3.4 %copy-start.1 = (bf16[1,1024,1024]{2,1,0:T(8,128)(2,1)S(1)}, bf16[1,1024,1024]{2,1,0:T(8,128)(2,1)}, u32[]{:S(2)}) copy-start(bf16[1,1024,1024]{2,1,0:T(8,128)(2,1)} %param.4) | copy-start | bytes 6291460
  63.8 2.4 copy-start.5
  74.1 160.9 %collective-permute-start.9 = (bf16[256,1024]{1,0:T(8,128)(2,1)S(1)}, bf16[256,1024]{1,0:T(8,128)(2,1)S(1)}, u32[]{:S(2)}, u32[]{:S(2)}) collective-permute-start(bf16[256,1024]{1,0:T(8,128)(2,1)S(1)} %collective-permute-done.2), channel_id=1, source_target_pairs={{0,8},{8,0},{1,9},{9,1},{2,10},{10,2},{3,11},{11,3},{4,12},{12,4},... | collective-permute-start | bytes 1572872 | tf_op jit(solution)/shard_map/ppermute | solution.py:226
  75.2 159.8 %collective-permute-start.10 = (bf16[256,1024]{1,0:T(8,128)(2,1)S(1)}, bf16[256,1024]{1,0:T(8,128)(2,1)S(1)}, u32[]{:S(2)}, u32[]{:S(2)}) collective-permute-start(bf16[256,1024]{1,0:T(8,128)(2,1)S(1)} %collective-permute-done.3), channel_id=1, source_target_pairs={{0,8},{8,0},{1,9},{9,1},{2,10},{10,2},{3,11},{11,3},{4,12},{12,4},... | collective-permute-start | bytes 1572872 | tf_op jit(solution)/shard_map/ppermute | solution.py:226
  76.7 158.3 %collective-permute-start.11 = (bf16[256,1024]{1,0:T(8,128)(2,1)S(1)}, bf16[256,1024]{1,0:T(8,128)(2,1)S(1)}, u32[]{:S(2)}, u32[]{:S(2)}) collective-permute-start(bf16[256,1024]{1,0:T(8,128)(2,1)S(1)} %collective-permute-done.4), channel_id=1, source_target_pairs={{0,8},{8,0},{1,9},{9,1},{2,10},{10,2},{3,11},{11,3},{4,12},{12,4},... | collective-permute-start | bytes 1572872 | tf_op jit(solution)/shard_map/ppermute | solution.py:226
  80.9 9.1 %collective-permute-start.5 = (bf16[512,1024]{1,0:T(8,128)(2,1)S(1)}, bf16[512,1024]{1,0:T(8,128)(2,1)S(1)}, u32[]{:S(2)}, u32[]{:S(2)}) collective-permute-start(bf16[512,1024]{1,0:T(8,128)(2,1)S(1)} %maximum_select_fusion), channel_id=1, source_target_pairs={{0,1},{1,0},{2,3},{3,2},{4,5},{5,4},{6,7},{7,6},{8,9},{9,8},{10,11... | collective-permute-start | bytes 3145736 | tf_op jit(solution)/shard_map/ppermute | solution.py:227
  90.1 149.3 %collective-permute-start.6 = (bf16[768,1024]{1,0:T(8,128)(2,1)S(1)}, bf16[768,1024]{1,0:T(8,128)(2,1)S(1)}, u32[]{:S(2)}, u32[]{:S(2)}) collective-permute-start(bf16[768,1024]{1,0:T(8,128)(2,1)S(1)} %constant_dynamic-update-slice_fusion), channel_id=1, source_target_pairs={{0,1},{1,0},{2,3},{3,2},{4,5},{5,4},{6,7},{7,6},{8,9},{9,8},{10,11... | collective-permute-start | bytes 4718600 | tf_op jit(solution)/shard_map/ppermute | solution.py:227
  235.1 7.9 %collective-permute-start.12 = (bf16[768,1024]{1,0:T(8,128)(2,1)S(1)}, bf16[768,1024]{1,0:T(8,128)(2,1)S(1)}, u32[]{:S(2)}, u32[]{:S(2)}) collective-permute-start(bf16[768,1024]{1,0:T(8,128)(2,1)S(1)} %constant_dynamic-update-slice_fusion.3), channel_id=1, source_target_pairs={{0,1},{1,0},{2,3},{3,2},{4,5},{5,4},{6,7},{7,6},{8,9},{9,8},{10,11... | collective-permute-start | bytes 4718600 | tf_op jit(solution)/shard_map/ppermute | solution.py:227
where the time goes:
time: 296 us; the launch traced here: 295 us
  Pallas kernels  192 us (65%)
  matrix products  45.4 us (15%)
  waiting for transfers between devices  29.9 us (10%)
  starting transfers between devices  20.6 us (7%)
  local copies, waits for them, and re-layouts  5.26 us (2%)
    pallas_call x2, Pallas kernels, attend(): pl.pallas_call(functools.partial(attend_kernel, not state, last, blocks,...  183 us
    dot_general x12, matrix products, project_columns(): lax.dot_general(weight, rows, (((1,), (1,)), ((), ())), preferred_element...  23 us
    dot_general x11, matrix products, project_rows(): jnp.dot(rows, weight, preferred_element_type=jnp.float32)  18.8 us
    ppermute x5, waiting for transfers between devices, rows_by_axes(): swap = lambda rows: lax.ppermute(rows, 'head', [(0, 1), (1, 0)])  18.6 us
    ppermute x2, starting transfers between devices, rows_by_axes(): to_next = lambda rows: lax.ppermute(rows, ('head', 'blk'), steps)  10.6 us
    pallas_call x1, Pallas kernels, split_weights(): pl.pallas_call(split_kernel, grid=(PAIRS,), in_specs=[pl.BlockSpec((D, 3...  8.61 us
  transfers between devices with their start and end apart: 13, of which 4 were waited for; matrix products, arithmetic and copies ran while one was open for 14% of the time, Pallas kernels for 50%

commit v1 on v0

--- a/solution.py
+++ b/solution.py
@@ -238,22 +238,25 @@
     other_end, own, weights = lax.optimization_barrier((other_end, own, weights))
     carried = jnp.where(low, other_end, own[cut : cut + half])
     other = swap(own[:-half])
-    slots = [along(carried, k) for k in range(1, chips)]
     edge_end = to_next(other_end)
-    own, other, other_end = lax.optimization_barrier((own, other, other_end))
+    ends = {1, chips - 1}
+    slots = {k: along(carried, k) for k in ends}
+    slots, after, own, other_end = lax.optimization_barrier((slots, carried, own, other_end))
+    middle = {k: along(after, k) for k in range(2, chips - 1)}
     query = project_columns(weights[0], own, HD**-0.5)
-    query, *slots = lax.optimization_barrier((query, *slots))
-    across = [swap(rows) for rows in slots]
+    across = {k: swap(slots[k]) for k in ends}
+    middle, other = lax.optimization_barrier((middle, other))
+    edge = to_next(other)
+    last, edge = lax.optimization_barrier(({k: swap(rows) for k, rows in middle.items()}, edge))
+    slots.update(middle)
+    across.update(last)
+    across = [across[k] for k in range(1, chips)]
+    slots = [slots[k] for k in range(1, chips)]
     foreign = jnp.concatenate(slots, axis=0)
     nearby = jnp.where(low, jnp.concatenate([other_end, other[-half:]], axis=0), own[cut:])
-    near_rows = [own, other, other_end, to_next(other), edge_end]
-    far_rows = [nearby, beside(nearby), foreign, beside(foreign)]
+    pieces = [own, other, other_end, edge, edge_end, beside(nearby), foreign, beside(foreign)]
+    pieces += across + [beside(rows) for rows in across]
     span = 2 * (chips - 1)
-
-    def late_rows(state):
-        state, arrived = lax.optimization_barrier((state, across))
-        arrived = jnp.concatenate(arrived, axis=0)
-        return state, [arrived, beside(arrived)]
 
     def position(block):
         of, inside = block // SB, block % SB
@@ -263,12 +266,11 @@
         order = inside - (SB - SUMB)
         k = (stride // 2 - of // 2) % chips
         turned = (order // 2 ^ (1 - place)) * 2 + order % 2
-        beside_me = jnp.where(of % 2 == stride % 2, 0, 1)
-        part = beside_me + jnp.where(order // 2 == 1 - place, 0, 2)
-        far = jnp.where(k == 0, 4 * beside_me + turned, 8 + part * span + (k - 1) * 2 + order % 2)
-        return jnp.where(of == stride, mine, edge), far
-
-    return near_rows, far_rows, late_rows, weights, query, position
+        part = jnp.where(of % 2 == stride % 2, 0, 1) + jnp.where(order // 2 == 1 - place, 0, 2)
+        far = jnp.where(k == 0, 24 + turned, 28 + part * span + (k - 1) * 2 + order % 2)
+        return jnp.where(of == stride, mine, edge), jnp.where(of == stride, mine, far)
+
+    return pieces, weights, query, position
 
 
 def rows_by_gather(own, place, stride, strides, heads):
@@ -289,9 +291,9 @@
     def position(block):
         rel = block - stride * SB
         near = jnp.where(rel < 0, rel + SB + REACH, rel)
-        return near, block // SB * SUMB + block % SB - (SB - SUMB)
-
-    return [stride_rows, edge], [far_rows], lambda state: (state, []), position
+        return near, SB + REACH + block // SB * SUMB + block % SB - (SB - SUMB)
+
+    return [stride_rows, edge, far_rows], position
 
 
 def on_device(tokens, proj_weight, out_weight, pattern):
@@ -304,27 +306,18 @@
     weights = split_weights(proj_weight)
 
     if heads == 2:
-        near_rows, far_rows, late_rows, weights, query, position = rows_by_axes(
-            own, weights, place, stride, strides
-        )
+        pieces, weights, query, position = rows_by_axes(own, weights, place, stride, strides)
     else:
-        near_rows, far_rows, late_rows, position = rows_by_gather(own, place, stride, strides, heads)
+        pieces, position = rows_by_gather(own, place, stride, strides, heads)
         query = project_columns(weights[0], own, HD**-0.5)
     listed = lax.dynamic_slice_in_dim(pattern, place * blocks, blocks, 0)
-    near = position(listed[:, :LSEL])[0]
-    far = position(listed[:, LSEL:])[1]
+    near, far = position(listed)
+    table = jnp.where(lax.broadcasted_iota(jnp.int32, listed.shape, 1) < LSEL, near, far)
 
     _, key_weight, value_weight = weights
-    both = lambda pieces: (
-        [project_rows(rows, key_weight) for rows in pieces],
-        [project_columns(value_weight, rows) for rows in pieces],
-    )
-    near_keys, near_values = both(near_rows)
-    far_keys, far_values = both(far_rows)
-    state = attend("attend_near", near, query, near_keys, near_values, [], False, 2, 4)
-    state, late = late_rows(state)
-    late_keys, late_values = both(late)
-    mixed = attend("attend_far", far, query, far_keys + late_keys, far_values + late_values, state, True, 2, 4)
+    keys = [project_rows(rows, key_weight) for rows in pieces]
+    values = [project_columns(value_weight, rows) for rows in pieces]
+    mixed = attend("attend", table, query, keys, values, [], True, 2, 4)
     out = jnp.dot(mixed, out_weight, preferred_element_type=jnp.float32).astype(jnp.bfloat16)
     return out.reshape(tokens.shape)
 

time: 296 us -> 471 us (1.59)
  Pallas kernels: 192 us -> 352 us
  waiting for transfers between devices: 29.9 us -> 52.4 us
  matrix products: 45.4 us -> 39.9 us
    pallas_call x2 -> x1, Pallas kernels: 183 us -> 343 us  [attend(): pl.pallas_call(functools.partial(attend_kernel, not state, last, blocks,...]
    ppermute x3, waiting for transfers between devices: 5.4 us -> 17 us  [along(): lax.ppermute(rows, 'blk', [(s, (s + 2 * k) % strides) for s in range(stri...]
    ppermute x5, waiting for transfers between devices: 18.6 us -> 29.6 us  [rows_by_axes(): swap = lambda rows: lax.ppermute(rows, 'head', [(0, 1), (1, 0)])]
    dot_general x12 -> x15, matrix products: 23 us -> 19.5 us  [project_columns(): lax.dot_general(weight, rows, (((1,), (1,)), ((), ())), preferred_element...]
    dot_general x11 -> x14, matrix products: 18.8 us -> 16.7 us  [project_rows(): jnp.dot(rows, weight, preferred_element_type=jnp.float32)]
  transfers between devices with their start and end apart: 13 -> 15, of which waited for: 4 -> 6; matrix products, arithmetic and copies ran while one was open for 14% -> 8% of each run, Pallas kernels for 50% -> 2%
where the time goes in v1:
time: 471 us; the launch traced here: 469 us
  Pallas kernels  352 us (75%)
  waiting for transfers between devices  52.4 us (11%)
  matrix products  39.9 us (8%)
  starting transfers between devices  16.9 us (4%)
  local copies, waits for them, and re-layouts  4.81 us (1%)
    pallas_call x1, Pallas kernels, attend(): pl.pallas_call(functools.partial(attend_kernel, not state, last, blocks,...  343 us
    ppermute x5, waiting for transfers between devices, rows_by_axes(): swap = lambda rows: lax.ppermute(rows, 'head', [(0, 1), (1, 0)])  29.6 us
    dot_general x15, matrix products, project_columns(): lax.dot_general(weight, rows, (((1,), (1,)), ((), ())), preferred_element...  19.5 us
    ppermute x3, waiting for transfers between devices, along(): lax.ppermute(rows, 'blk', [(s, (s + 2 * k) % strides) for s in range(stri...  17 us
    dot_general x14, matrix products, project_rows(): jnp.dot(rows, weight, preferred_element_type=jnp.float32)  16.7 us
  transfers between devices with their start and end apart: 15, of which 6 were waited for; matrix products, arithmetic and copies ran while one was open for 8% of the time, Pallas kernels for 2%

profile of v1, /device:TPU:11, one launch (start us, length us, event | category | flops | bytes accessed | tf_op | source)
XLA Modules:
  0.0 469.0 jit_solution(14254232117249488710)
XLA Ops:
  0.0 1.2 slice_bitcast_fusion
  1.2 1.3 collective-permute-start
  2.5 8.6 %split_weights.1 = (bf16[1024,1024]{1,0:T(8,128)(2,1)}, bf16[1024,1024]{1,0:T(8,128)(2,1)}, bf16[1024,1024]{1,0:T(8,128)(2,1)}) custom-call(bf16[1024,3072]{1,0:T(8,128)(2,1)} %weight_ref.1), custom_call_target="tpu_custom_call" | custom-call | bytes 12582912 | tf_op jit(solution)/shard_map/split_weights/pallas_call | solution.py:41
  11.1 2.9 collective-permute-done
  14.1 1.9 slice_select_fusion
  16.2 1.3 collective-permute-start.1
  17.5 5.3 %collective-permute-start.7 = (bf16[256,1024]{1,0:T(8,128)(2,1)S(1)}, bf16[256,1024]{1,0:T(8,128)(2,1)S(1)}, u32[]{:S(2)}, u32[]{:S(2)}) collective-permute-start(bf16[256,1024]{1,0:T(8,128)(2,1)S(1)} %collective-permute-done), channel_id=1, source_target_pairs={{0,1},{9,8},{1,2},{10,9},{2,3},{11,10},{3,4},{12,11},{4,5},{13,12}... | collective-permute-start | bytes 1572872 | tf_op jit(solution)/shard_map/ppermute | solution.py:235
  22.9 1.5 slice.21
  24.5 3.6 collective-permute-done.2
  28.1 13.5 %collective-permute-done.1 = bf16[256,1024]{1,0:T(8,128)(2,1)} collective-permute-done((bf16[256,1024]{1,0:T(8,128)(2,1)}, bf16[256,1024]{1,0:T(8,128)(2,1)}, u32[]{:S(2)}, u32[]{:S(2)}) %collective-permute-start.1) | collective-permute-done | bytes 524320 | tf_op jit(solution)/shard_map/ppermute | solution.py:230
  43.9 2.3 convolution_convert_fusion.1.refs_2_
  46.3 2.4 convolution_convert_fusion.refs_16_
  49.3 1.2 collective-permute-start.10
  50.8 2.4 multiply_convert_fusion.refs_1_
  55.7 16.4 %collective-permute-done.10 = bf16[256,1024]{1,0:T(8,128)(2,1)S(1)} collective-permute-done((bf16[256,1024]{1,0:T(8,128)(2,1)}, bf16[256,1024]{1,0:T(8,128)(2,1)S(1)}, u32[]{:S(2)}, u32[]{:S(2)}) %collective-permute-start.10) | collective-permute-done | bytes 524320 | tf_op jit(solution)/shard_map/ppermute | solution.py:226
  72.1 10.3 %collective-permute-done.11 = bf16[256,1024]{1,0:T(8,128)(2,1)S(1)} collective-permute-done((bf16[256,1024]{1,0:T(8,128)(2,1)S(1)}, bf16[256,1024]{1,0:T(8,128)(2,1)S(1)}, u32[]{:S(2)}, u32[]{:S(2)}) %collective-permute-start.11) | collective-permute-done | bytes 524320 | tf_op jit(solution)/shard_map/ppermute | solution.py:226
  85.4 1.5 collective-permute-start.5
  86.9 2.0 convolution_convert_fusion.3.refs_22_
  89.4 3.4 collective-permute-start.6
  93.2 1.8 convolution_convert_fusion.7.refs_8_
  96.6 1.8 convolution_convert_fusion.5.refs_17_
  99.9 1.8 convolution_convert_fusion.9.refs_3_
  101.7 1.3 convolution_convert_fusion.10.refs_21_
  103.0 1.3 convolution_convert_fusion.11.refs_7_
  104.3 5.8 %collective-permute-done.6 = bf16[768,1024]{1,0:T(8,128)(2,1)S(1)} collective-permute-done((bf16[768,1024]{1,0:T(8,128)(2,1)S(1)}, bf16[768,1024]{1,0:T(8,128)(2,1)S(1)}, u32[]{:S(2)}, u32[]{:S(2)}) %collective-permute-start.6) | collective-permute-done | bytes 1572896 | tf_op jit(solution)/shard_map/ppermute | solution.py:235
  110.1 1.2 collective-permute-start.13
  112.1 1.8 convolution_convert_fusion.4.refs_19_
  113.9 2.0 convolution_convert_fusion.8.refs_5_
  116.0 1.8 convolution_convert_fusion.2.refs_23_
  118.5 1.8 convolution_convert_fusion.6.refs_9_
  121.8 343.5 %attend.1 = bf16[1024,1024]{1,0:T(8,128)(2,1)S(1)} custom-call(s32[8,16]{1,0:T(8,128)S(1)} %fusion.6.refs_0_, bf16[1024,1024]{1,0:T(8,128)(2,1)S(1)} %multiply_convert_fusion.refs_1_, bf16[1024,1024]{1,0:T(8,128)(2,1)S(1)} %convolution_convert_fusion.1.refs_2_, bf16[768,1024]{1,0:T(8,128)(2,1)S(1)} %convolution_convert_fusion.9.refs_3_, ...), custom_call_target="tpu_custom_call" | custom-call | flops 51539607552 | bytes 37748736 | tf_op jit(solution)/shard_map/attend/pallas_call | solution.py:196
  465.3 3.7 convert_bitcast_fusion
  (52 shorter events, 15.9 us)
Async XLA Ops:
  0.0 465.3 %copy-start = (bf16[1024,1024]{1,0:T(8,128)(2,1)S(1)}, bf16[1024,1024]{1,0:T(8,128)(2,1)}, u32[]{:S(2)}) copy-start(bf16[1024,1024]{1,0:T(8,128)(2,1)} %param.6) | copy-start | bytes 6291460
  1.2 12.9 %collective-permute-start = (bf16[256,1024]{1,0:T(8,128)(2,1)S(1)}, bf16[256,1024]{1,0:T(8,128)(2,1)S(1)}, u32[]{:S(2)}, u32[]{:S(2)}) collective-permute-start(bf16[256,1024]{1,0:T(8,128)(2,1)S(1)} %slice_bitcast_fusion), channel_id=1, source_target_pairs={{0,8},{8,0},{1,9},{9,1},{2,10},{10,2},{3,11},{11,3},{4,12},{12,4},... | collective-permute-start | bytes 1572872 | tf_op jit(solution)/shard_map/ppermute | solution.py:226
  2.5 15.0 %copy-start.2 = (s32[16,16]{1,0:T(8,128)S(1)}, s32[16,16]{1,0:T(8,128)}, u32[]{:S(2)}) copy-start(s32[16,16]{1,0:T(8,128)} %param.7) | copy-start | bytes 3076
  16.0 12.1 %collective-permute-start.2 = (bf16[256,1024]{1,0:T(8,128)(2,1)}, bf16[256,1024]{1,0:T(8,128)(2,1)S(1)}, u32[]{:S(2)}, u32[]{:S(2)}) collective-permute-start(bf16[256,1024]{1,0:T(8,128)(2,1)} %slice_select_fusion), channel_id=1, source_target_pairs={{0,6},{1,7},{2,0},{3,1},{4,2},{5,3},{6,4},{7,5},{8,14},{9,15},{10,... | collective-permute-start | bytes 1572872 | tf_op jit(solution)/shard_map/ppermute | solution.py:230
  16.2 25.4 %collective-permute-start.1 = (bf16[256,1024]{1,0:T(8,128)(2,1)}, bf16[256,1024]{1,0:T(8,128)(2,1)}, u32[]{:S(2)}, u32[]{:S(2)}) collective-permute-start(bf16[256,1024]{1,0:T(8,128)(2,1)} %slice_select_fusion), channel_id=1, source_target_pairs={{0,2},{1,3},{2,4},{3,5},{4,6},{5,7},{6,0},{7,1},{8,10},{9,11},{10,... | collective-permute-start | bytes 1572872 | tf_op jit(solution)/shard_map/ppermute | solution.py:230
  17.5 24.1 %copy-start.4 = (bf16[1024,1024]{1,0:T(8,128)(2,1)S(1)}, bf16[1024,1024]{1,0:T(8,128)(2,1)}, u32[]{:S(2)}) copy-start(bf16[1024,1024]{1,0:T(8,128)(2,1)} %get-tuple-element.38) | copy-start | bytes 6291460
  17.5 35.6 %collective-permute-start.7 = (bf16[256,1024]{1,0:T(8,128)(2,1)S(1)}, bf16[256,1024]{1,0:T(8,128)(2,1)S(1)}, u32[]{:S(2)}, u32[]{:S(2)}) collective-permute-start(bf16[256,1024]{1,0:T(8,128)(2,1)S(1)} %collective-permute-done), channel_id=1, source_target_pairs={{0,1},{9,8},{1,2},{10,9},{2,3},{11,10},{3,4},{12,11},{4,5},{13,12}... | collective-permute-start | bytes 1572872 | tf_op jit(solution)/shard_map/ppermute | solution.py:235
  24.4 17.9 %copy-start.3 = (bf16[1024,1024]{1,0:T(8,128)(2,1)S(1)}, bf16[1024,1024]{1,0:T(8,128)(2,1)}, u32[]{:S(2)}) copy-start(bf16[1024,1024]{1,0:T(8,128)(2,1)} %get-tuple-element.29) | copy-start | bytes 6291460
  24.4 60.9 %collective-permute-start.4 = (bf16[768,1024]{1,0:T(8,128)(2,1)S(1)}, bf16[768,1024]{1,0:T(8,128)(2,1)S(1)}, u32[]{:S(2)}, u32[]{:S(2)}) collective-permute-start(bf16[768,1024]{1,0:T(8,128)(2,1)S(1)} %slice.21), channel_id=1, source_target_pairs={{0,8},{8,0},{1,9},{9,1},{2,10},{10,2},{3,11},{11,3},{4,12},{12,4},... | collective-permute-start | bytes 4718600 | tf_op jit(solution)/shard_map/ppermute | solution.py:226
  42.3 1.6 copy-start.1
  46.3 4.5 copy-start.5
  48.7 36.7 %collective-permute-start.3 = (bf16[256,1024]{1,0:T(8,128)(2,1)}, bf16[256,1024]{1,0:T(8,128)(2,1)S(1)}, u32[]{:S(2)}, u32[]{:S(2)}) collective-permute-start(bf16[256,1024]{1,0:T(8,128)(2,1)} %slice_select_fusion), channel_id=1, source_target_pairs={{0,4},{1,5},{2,6},{3,7},{4,0},{5,1},{6,2},{7,3},{8,12},{9,13},{10,... | collective-permute-start | bytes 1572872 | tf_op jit(solution)/shard_map/ppermute | solution.py:230
  49.3 22.8 %collective-permute-start.10 = (bf16[256,1024]{1,0:T(8,128)(2,1)}, bf16[256,1024]{1,0:T(8,128)(2,1)S(1)}, u32[]{:S(2)}, u32[]{:S(2)}) collective-permute-start(bf16[256,1024]{1,0:T(8,128)(2,1)} %collective-permute-done.1), channel_id=1, source_target_pairs={{0,8},{8,0},{1,9},{9,1},{2,10},{10,2},{3,11},{11,3},{4,12},{12,4},... | collective-permute-start | bytes 1572872 | tf_op jit(solution)/shard_map/ppermute | solution.py:226
  50.5 31.8 %collective-permute-start.11 = (bf16[256,1024]{1,0:T(8,128)(2,1)S(1)}, bf16[256,1024]{1,0:T(8,128)(2,1)S(1)}, u32[]{:S(2)}, u32[]{:S(2)}) collective-permute-start(bf16[256,1024]{1,0:T(8,128)(2,1)S(1)} %collective-permute-done.2), channel_id=1, source_target_pairs={{0,8},{8,0},{1,9},{9,1},{2,10},{10,2},{3,11},{11,3},{4,12},{12,4},... | collective-permute-start | bytes 1572872 | tf_op jit(solution)/shard_map/ppermute | solution.py:226
  72.1 22.9 %collective-permute-start.12 = (bf16[256,1024]{1,0:T(8,128)(2,1)S(1)}, bf16[256,1024]{1,0:T(8,128)(2,1)S(1)}, u32[]{:S(2)}, u32[]{:S(2)}) collective-permute-start(bf16[256,1024]{1,0:T(8,128)(2,1)S(1)} %collective-permute-done.10), channel_id=1, source_target_pairs={{0,1},{1,0},{2,3},{3,2},{4,5},{5,4},{6,7},{7,6},{8,9},{9,8},{10,11... | collective-permute-start | bytes 1572872 | tf_op jit(solution)/shard_map/ppermute | solution.py:227
  82.4 16.0 %collective-permute-start.14 = (bf16[256,1024]{1,0:T(8,128)(2,1)S(1)}, bf16[256,1024]{1,0:T(8,128)(2,1)S(1)}, u32[]{:S(2)}, u32[]{:S(2)}) collective-permute-start(bf16[256,1024]{1,0:T(8,128)(2,1)S(1)} %collective-permute-done.11), channel_id=1, source_target_pairs={{0,1},{1,0},{2,3},{3,2},{4,5},{5,4},{6,7},{7,6},{8,9},{9,8},{10,11... | collective-permute-start | bytes 1572872 | tf_op jit(solution)/shard_map/ppermute | solution.py:227
  85.4 18.9 %collective-permute-start.5 = (bf16[256,1024]{1,0:T(8,128)(2,1)S(1)}, bf16[256,1024]{1,0:T(8,128)(2,1)S(1)}, u32[]{:S(2)}, u32[]{:S(2)}) collective-permute-start(bf16[256,1024]{1,0:T(8,128)(2,1)S(1)} %collective-permute-done.3), channel_id=1, source_target_pairs={{0,8},{8,0},{1,9},{9,1},{2,10},{10,2},{3,11},{11,3},{4,12},{12,4},... | collective-permute-start | bytes 1572872 | tf_op jit(solution)/shard_map/ppermute | solution.py:226
  89.0 27.0 %collective-permute-start.9 = (bf16[768,1024]{1,0:T(8,128)(2,1)S(1)}, bf16[768,1024]{1,0:T(8,128)(2,1)S(1)}, u32[]{:S(2)}, u32[]{:S(2)}) collective-permute-start(bf16[768,1024]{1,0:T(8,128)(2,1)S(1)} %constant_dynamic-update-slice_fusion), channel_id=1, source_target_pairs={{0,1},{1,0},{2,3},{3,2},{4,5},{5,4},{6,7},{7,6},{8,9},{9,8},{10,11... | collective-permute-start | bytes 4718600 | tf_op jit(solution)/shard_map/ppermute | solution.py:227
  89.4 20.7 %collective-permute-start.6 = (bf16[768,1024]{1,0:T(8,128)(2,1)S(1)}, bf16[768,1024]{1,0:T(8,128)(2,1)S(1)}, u32[]{:S(2)}, u32[]{:S(2)}) collective-permute-start(bf16[768,1024]{1,0:T(8,128)(2,1)S(1)} %collective-permute-done.4), channel_id=1, source_target_pairs={{0,1},{9,8},{1,2},{10,9},{2,3},{11,10},{3,4},{12,11},{4,5},{13,12}... | collective-permute-start | bytes 4718600 | tf_op jit(solution)/shard_map/ppermute | solution.py:235
  95.0 6.7 %collective-permute-start.8 = (bf16[512,1024]{1,0:T(8,128)(2,1)S(1)}, bf16[512,1024]{1,0:T(8,128)(2,1)S(1)}, u32[]{:S(2)}, u32[]{:S(2)}) collective-permute-start(bf16[512,1024]{1,0:T(8,128)(2,1)S(1)} %maximum_select_fusion), channel_id=1, source_target_pairs={{0,1},{1,0},{2,3},{3,2},{4,5},{5,4},{6,7},{7,6},{8,9},{9,8},{10,11... | collective-permute-start | bytes 3145736 | tf_op jit(solution)/shard_map/ppermute | solution.py:227
  110.1 10.2 %collective-permute-start.13 = (bf16[256,1024]{1,0:T(8,128)(2,1)S(1)}, bf16[256,1024]{1,0:T(8,128)(2,1)S(1)}, u32[]{:S(2)}, u32[]{:S(2)}) collective-permute-start(bf16[256,1024]{1,0:T(8,128)(2,1)S(1)} %collective-permute-done.5), channel_id=1, source_target_pairs={{0,1},{1,0},{2,3},{3,2},{4,5},{5,4},{6,7},{7,6},{8,9},{9,8},{10,11... | collective-permute-start | bytes 1572872 | tf_op jit(solution)/shard_map/ppermute | solution.py:227

commit v2 on v1

--- a/solution.py
+++ b/solution.py
@@ -239,19 +239,12 @@
     carried = jnp.where(low, other_end, own[cut : cut + half])
     other = swap(own[:-half])
     edge_end = to_next(other_end)
-    ends = {1, chips - 1}
-    slots = {k: along(carried, k) for k in ends}
-    slots, after, own, other_end = lax.optimization_barrier((slots, carried, own, other_end))
-    middle = {k: along(after, k) for k in range(2, chips - 1)}
+    slots = [along(carried, k) for k in range(1, chips)]
+    own, other, other_end = lax.optimization_barrier((own, other, other_end))
     query = project_columns(weights[0], own, HD**-0.5)
-    across = {k: swap(slots[k]) for k in ends}
-    middle, other = lax.optimization_barrier((middle, other))
     edge = to_next(other)
-    last, edge = lax.optimization_barrier(({k: swap(rows) for k, rows in middle.items()}, edge))
-    slots.update(middle)
-    across.update(last)
-    across = [across[k] for k in range(1, chips)]
-    slots = [slots[k] for k in range(1, chips)]
+    query, *slots = lax.optimization_barrier((query, *slots))
+    across, edge = lax.optimization_barrier(([swap(rows) for rows in slots], edge))
     foreign = jnp.concatenate(slots, axis=0)
     nearby = jnp.where(low, jnp.concatenate([other_end, other[-half:]], axis=0), own[cut:])
     pieces = [own, other, other_end, edge, edge_end, beside(nearby), foreign, beside(foreign)]
@@ -317,7 +310,7 @@
     _, key_weight, value_weight = weights
     keys = [project_rows(rows, key_weight) for rows in pieces]
     values = [project_columns(value_weight, rows) for rows in pieces]
-    mixed = attend("attend", table, query, keys, values, [], True, 2, 4)
+    mixed = attend("attend", table, query, keys, values, [], True, 2, 8)
     out = jnp.dot(mixed, out_weight, preferred_element_type=jnp.float32).astype(jnp.bfloat16)
     return out.reshape(tokens.shape)
 

time: 471 us -> 475 us (level)
    ppermute x2, waiting for transfers between devices: 5.84 us -> 26.9 us  [rows_by_axes(): to_next = lambda rows: lax.ppermute(rows, ('head', 'blk'), steps)]
    ppermute x5, waiting for transfers between devices: 29.6 us -> 11.3 us  [rows_by_axes(): swap = lambda rows: lax.ppermute(rows, 'head', [(0, 1), (1, 0)])]
  transfers between devices with their start and end apart: 15 -> 15, of which waited for: 6 -> 5; matrix products, arithmetic and copies ran while one was open for 8% -> 9% of each run, Pallas kernels for 2% -> 2%
where the time goes in v2:
time: 475 us; the launch traced here: 474 us
  Pallas kernels  353 us (74%)
  waiting for transfers between devices  52.1 us (11%)
  matrix products  44.3 us (9%)
  starting transfers between devices  16.5 us (3%)
  local copies, waits for them, and re-layouts  5.98 us (1%)
    pallas_call x1, Pallas kernels, attend(): pl.pallas_call(functools.partial(attend_kernel, not state, last, blocks,...  344 us
    ppermute x2, waiting for transfers between devices, rows_by_axes(): to_next = lambda rows: lax.ppermute(rows, ('head', 'blk'), steps)  26.9 us
    dot_general x15, matrix products, project_columns(): lax.dot_general(weight, rows, (((1,), (1,)), ((), ())), preferred_element...  22.7 us
    dot_general x14, matrix products, project_rows(): jnp.dot(rows, weight, preferred_element_type=jnp.float32)  17.9 us
    ppermute x3, waiting for transfers between devices, along(): lax.ppermute(rows, 'blk', [(s, (s + 2 * k) % strides) for s in range(stri...  13.9 us
    ppermute x5, waiting for transfers between devices, rows_by_axes(): swap = lambda rows: lax.ppermute(rows, 'head', [(0, 1), (1, 0)])  11.3 us
  transfers between devices with their start and end apart: 15, of which 5 were waited for; matrix products, arithmetic and copies ran while one was open for 9% of the time, Pallas kernels for 2%

profile of v2, /device:TPU:11, one launch (start us, length us, event | category | flops | bytes accessed | tf_op | source)
XLA Modules:
  0.0 473.6 jit_solution(3321811329738729318)
XLA Ops:
  0.0 1.2 slice_bitcast_fusion
  1.2 1.3 collective-permute-start
  2.5 8.6 %split_weights.1 = (bf16[1024,1024]{1,0:T(8,128)(2,1)}, bf16[1024,1024]{1,0:T(8,128)(2,1)}, bf16[1024,1024]{1,0:T(8,128)(2,1)}) custom-call(bf16[1024,3072]{1,0:T(8,128)(2,1)} %weight_ref.1), custom_call_target="tpu_custom_call" | custom-call | bytes 12582912 | tf_op jit(solution)/shard_map/split_weights/pallas_call | solution.py:41
  11.1 2.9 collective-permute-done
  14.1 2.7 slice.20
  16.8 1.2 collective-permute-start.1
  18.0 4.9 %collective-permute-start.9 = (bf16[256,1024]{1,0:T(8,128)(2,1)S(1)}, bf16[256,1024]{1,0:T(8,128)(2,1)S(1)}, u32[]{:S(2)}, u32[]{:S(2)}) collective-permute-start(bf16[256,1024]{1,0:T(8,128)(2,1)S(1)} %collective-permute-done), channel_id=1, source_target_pairs={{0,1},{9,8},{1,2},{10,9},{2,3},{11,10},{3,4},{12,11},{4,5},{13,12}... | collective-permute-start | bytes 1572872 | tf_op jit(solution)/shard_map/ppermute | solution.py:235
  23.0 1.1 slice_select_fusion
  24.4 2.3 collective-permute-start.3
  26.7 26.9 %collective-permute-done.9 = bf16[256,1024]{1,0:T(8,128)(2,1)S(1)} collective-permute-done((bf16[256,1024]{1,0:T(8,128)(2,1)S(1)}, bf16[256,1024]{1,0:T(8,128)(2,1)S(1)}, u32[]{:S(2)}, u32[]{:S(2)}) %collective-permute-start.9) | collective-permute-done | bytes 524320 | tf_op jit(solution)/shard_map/ppermute | solution.py:235
  53.6 2.5 convolution_convert_fusion.18.refs_20_
  57.7 2.4 multiply_convert_fusion.refs_1_
  60.1 4.9 %collective-permute-done.3 = bf16[256,1024]{1,0:T(8,128)(2,1)S(1)} collective-permute-done((bf16[256,1024]{1,0:T(8,128)(2,1)S(1)}, bf16[256,1024]{1,0:T(8,128)(2,1)S(1)}, u32[]{:S(2)}, u32[]{:S(2)}) %collective-permute-start.3) | collective-permute-done | bytes 524320 | tf_op jit(solution)/shard_map/ppermute | solution.py:230
  65.0 9.0 %collective-permute-done.2 = bf16[256,1024]{1,0:T(8,128)(2,1)S(1)} collective-permute-done((bf16[256,1024]{1,0:T(8,128)(2,1)S(1)}, bf16[256,1024]{1,0:T(8,128)(2,1)S(1)}, u32[]{:S(2)}, u32[]{:S(2)}) %collective-permute-start.2) | collective-permute-done | bytes 524320 | tf_op jit(solution)/shard_map/ppermute | solution.py:230
  74.1 1.5 collective-permute-start.6
  75.8 1.8 convolution_convert_fusion.3.refs_22_
  77.6 1.8 convolution_convert_fusion.7.refs_8_
  79.4 1.1 slice.22
  80.5 3.3 convolution_convert_fusion.5.refs_17_
  83.8 3.2 convolution_convert_fusion.9.refs_3_
  87.0 3.6 collective-permute-start.8
  90.6 2.3 convolution_convert_fusion.1.refs_2_
  95.0 2.4 convolution_convert_fusion.refs_16_
  97.9 1.3 convolution_convert_fusion.10.refs_21_
  99.2 1.3 convolution_convert_fusion.11.refs_7_
  100.5 8.3 %collective-permute-done.7 = bf16[256,1024]{1,0:T(8,128)(2,1)S(1)} collective-permute-done((bf16[256,1024]{1,0:T(8,128)(2,1)S(1)}, bf16[256,1024]{1,0:T(8,128)(2,1)S(1)}, u32[]{:S(2)}, u32[]{:S(2)}) %collective-permute-start.7) | collective-permute-done | bytes 524320 | tf_op jit(solution)/shard_map/ppermute | solution.py:226
  113.9 2.1 convolution_convert_fusion.4.refs_19_
  115.9 1.8 convolution_convert_fusion.2.refs_23_
  117.8 1.8 convolution_convert_fusion.8.refs_5_
  119.6 1.8 convolution_convert_fusion.6.refs_9_
  125.8 344.0 %attend.1 = bf16[1024,1024]{1,0:T(8,128)(2,1)S(1)} custom-call(s32[8,16]{1,0:T(8,128)S(1)} %fusion.6.refs_0_, bf16[1024,1024]{1,0:T(8,128)(2,1)S(1)} %multiply_convert_fusion.refs_1_, bf16[1024,1024]{1,0:T(8,128)(2,1)S(1)} %convolution_convert_fusion.1.refs_2_, bf16[768,1024]{1,0:T(8,128)(2,1)S(1)} %convolution_convert_fusion.9.refs_3_, ...), custom_call_target="tpu_custom_call" | custom-call | flops 51539607552 | bytes 37748736 | tf_op jit(solution)/shard_map/attend/pallas_call | solution.py:196
  469.9 3.7 convert_bitcast_fusion
  (52 shorter events, 14.0 us)
Async XLA Ops:
  0.0 469.9 %copy-start = (bf16[1024,1024]{1,0:T(8,128)(2,1)S(1)}, bf16[1024,1024]{1,0:T(8,128)(2,1)}, u32[]{:S(2)}) copy-start(bf16[1024,1024]{1,0:T(8,128)(2,1)} %param.6) | copy-start | bytes 6291460
  1.2 12.9 %collective-permute-start = (bf16[256,1024]{1,0:T(8,128)(2,1)S(1)}, bf16[256,1024]{1,0:T(8,128)(2,1)S(1)}, u32[]{:S(2)}, u32[]{:S(2)}) collective-permute-start(bf16[256,1024]{1,0:T(8,128)(2,1)S(1)} %slice_bitcast_fusion), channel_id=1, source_target_pairs={{0,8},{8,0},{1,9},{9,1},{2,10},{10,2},{3,11},{11,3},{4,12},{12,4},... | collective-permute-start | bytes 1572872 | tf_op jit(solution)/shard_map/ppermute | solution.py:226
  11.1 11.8 %copy-start.2 = (s32[16,16]{1,0:T(8,128)S(1)}, s32[16,16]{1,0:T(8,128)}, u32[]{:S(2)}) copy-start(s32[16,16]{1,0:T(8,128)} %param.7) | copy-start | bytes 3076
  16.8 40.0 %collective-permute-start.1 = (bf16[768,1024]{1,0:T(8,128)(2,1)}, bf16[768,1024]{1,0:T(8,128)(2,1)}, u32[]{:S(2)}, u32[]{:S(2)}) collective-permute-start(bf16[768,1024]{1,0:T(8,128)(2,1)} %slice.20), channel_id=1, source_target_pairs={{0,8},{8,0},{1,9},{9,1},{2,10},{10,2},{3,11},{11,3},{4,12},{12,4},... | collective-permute-start | bytes 4718600 | tf_op jit(solution)/shard_map/ppermute | solution.py:226
  18.0 35.6 %collective-permute-start.9 = (bf16[256,1024]{1,0:T(8,128)(2,1)S(1)}, bf16[256,1024]{1,0:T(8,128)(2,1)S(1)}, u32[]{:S(2)}, u32[]{:S(2)}) collective-permute-start(bf16[256,1024]{1,0:T(8,128)(2,1)S(1)} %collective-permute-done), channel_id=1, source_target_pairs={{0,1},{9,8},{1,2},{10,9},{2,3},{11,10},{3,4},{12,11},{4,5},{13,12}... | collective-permute-start | bytes 1572872 | tf_op jit(solution)/shard_map/ppermute | solution.py:235
  24.1 32.0 %copy-start.3 = (bf16[1024,1024]{1,0:T(8,128)(2,1)S(1)}, bf16[1024,1024]{1,0:T(8,128)(2,1)}, u32[]{:S(2)}) copy-start(bf16[1024,1024]{1,0:T(8,128)(2,1)} %get-tuple-element.32) | copy-start | bytes 6291460
  24.2 35.9 %collective-permute-start.4 = (bf16[256,1024]{1,0:T(8,128)(2,1)S(1)}, bf16[256,1024]{1,0:T(8,128)(2,1)S(1)}, u32[]{:S(2)}, u32[]{:S(2)}) collective-permute-start(bf16[256,1024]{1,0:T(8,128)(2,1)S(1)} %slice_select_fusion), channel_id=1, source_target_pairs={{0,6},{1,7},{2,0},{3,1},{4,2},{5,3},{6,4},{7,5},{8,14},{9,15},{10,... | collective-permute-start | bytes 1572872 | tf_op jit(solution)/shard_map/ppermute | solution.py:230
  24.4 40.7 %collective-permute-start.3 = (bf16[256,1024]{1,0:T(8,128)(2,1)S(1)}, bf16[256,1024]{1,0:T(8,128)(2,1)S(1)}, u32[]{:S(2)}, u32[]{:S(2)}) collective-permute-start(bf16[256,1024]{1,0:T(8,128)(2,1)S(1)} %slice_select_fusion), channel_id=1, source_target_pairs={{0,4},{1,5},{2,6},{3,7},{4,0},{5,1},{6,2},{7,3},{8,12},{9,13},{10,... | collective-permute-start | bytes 1572872 | tf_op jit(solution)/shard_map/ppermute | solution.py:230
  26.7 47.4 %collective-permute-start.2 = (bf16[256,1024]{1,0:T(8,128)(2,1)S(1)}, bf16[256,1024]{1,0:T(8,128)(2,1)S(1)}, u32[]{:S(2)}, u32[]{:S(2)}) collective-permute-start(bf16[256,1024]{1,0:T(8,128)(2,1)S(1)} %slice_select_fusion), channel_id=1, source_target_pairs={{0,2},{1,3},{2,4},{3,5},{4,6},{5,7},{6,0},{7,1},{8,10},{9,11},{10,... | collective-permute-start | bytes 1572872 | tf_op jit(solution)/shard_map/ppermute | solution.py:230
  53.6 3.3 copy-start.5
  56.1 1.6 copy-start.1
  60.1 15.7 %copy-start.4 = (bf16[1024,1024]{1,0:T(8,128)(2,1)S(1)}, bf16[1024,1024]{1,0:T(8,128)(2,1)}, u32[]{:S(2)}) copy-start(bf16[1024,1024]{1,0:T(8,128)(2,1)} %get-tuple-element.42) | copy-start | bytes 6291460
  74.0 26.4 %collective-permute-start.5 = (bf16[256,1024]{1,0:T(8,128)(2,1)S(1)}, bf16[256,1024]{1,0:T(8,128)(2,1)S(1)}, u32[]{:S(2)}, u32[]{:S(2)}) collective-permute-start(bf16[256,1024]{1,0:T(8,128)(2,1)S(1)} %collective-permute-done.2), channel_id=1, source_target_pairs={{0,8},{8,0},{1,9},{9,1},{2,10},{10,2},{3,11},{11,3},{4,12},{12,4},... | collective-permute-start | bytes 1572872 | tf_op jit(solution)/shard_map/ppermute | solution.py:226
  74.1 26.4 %collective-permute-start.6 = (bf16[256,1024]{1,0:T(8,128)(2,1)S(1)}, bf16[256,1024]{1,0:T(8,128)(2,1)S(1)}, u32[]{:S(2)}, u32[]{:S(2)}) collective-permute-start(bf16[256,1024]{1,0:T(8,128)(2,1)S(1)} %collective-permute-done.3), channel_id=1, source_target_pairs={{0,8},{8,0},{1,9},{9,1},{2,10},{10,2},{3,11},{11,3},{4,12},{12,4},... | collective-permute-start | bytes 1572872 | tf_op jit(solution)/shard_map/ppermute | solution.py:226
  75.6 33.2 %collective-permute-start.7 = (bf16[256,1024]{1,0:T(8,128)(2,1)S(1)}, bf16[256,1024]{1,0:T(8,128)(2,1)S(1)}, u32[]{:S(2)}, u32[]{:S(2)}) collective-permute-start(bf16[256,1024]{1,0:T(8,128)(2,1)S(1)} %collective-permute-done.4), channel_id=1, source_target_pairs={{0,8},{8,0},{1,9},{9,1},{2,10},{10,2},{3,11},{11,3},{4,12},{12,4},... | collective-permute-start | bytes 1572872 | tf_op jit(solution)/shard_map/ppermute | solution.py:226
  87.0 21.8 %collective-permute-start.8 = (bf16[768,1024]{1,0:T(8,128)(2,1)}, bf16[768,1024]{1,0:T(8,128)(2,1)S(1)}, u32[]{:S(2)}, u32[]{:S(2)}) collective-permute-start(bf16[768,1024]{1,0:T(8,128)(2,1)} %collective-permute-done.1), channel_id=1, source_target_pairs={{0,1},{9,8},{1,2},{10,9},{2,3},{11,10},{3,4},{12,11},{4,5},{13,12}... | collective-permute-start | bytes 4718600 | tf_op jit(solution)/shard_map/ppermute | solution.py:235
  93.4 3.9 collective-permute-start.10
  97.4 18.6 %collective-permute-start.11 = (bf16[768,1024]{1,0:T(8,128)(2,1)S(1)}, bf16[768,1024]{1,0:T(8,128)(2,1)S(1)}, u32[]{:S(2)}, u32[]{:S(2)}) collective-permute-start(bf16[768,1024]{1,0:T(8,128)(2,1)S(1)} %constant_dynamic-update-slice_fusion), channel_id=1, source_target_pairs={{0,1},{1,0},{2,3},{3,2},{4,5},{5,4},{6,7},{7,6},{8,9},{9,8},{10,11... | collective-permute-start | bytes 4718600 | tf_op jit(solution)/shard_map/ppermute | solution.py:227
  110.3 11.1 %collective-permute-start.12 = (bf16[256,1024]{1,0:T(8,128)(2,1)S(1)}, bf16[256,1024]{1,0:T(8,128)(2,1)S(1)}, u32[]{:S(2)}, u32[]{:S(2)}) collective-permute-start(bf16[256,1024]{1,0:T(8,128)(2,1)S(1)} %collective-permute-done.5), channel_id=1, source_target_pairs={{0,1},{1,0},{2,3},{3,2},{4,5},{5,4},{6,7},{7,6},{8,9},{9,8},{10,11... | collective-permute-start | bytes 1572872 | tf_op jit(solution)/shard_map/ppermute | solution.py:227
  110.3 12.5 %collective-permute-start.13 = (bf16[256,1024]{1,0:T(8,128)(2,1)S(1)}, bf16[256,1024]{1,0:T(8,128)(2,1)S(1)}, u32[]{:S(2)}, u32[]{:S(2)}) collective-permute-start(bf16[256,1024]{1,0:T(8,128)(2,1)S(1)} %collective-permute-done.6), channel_id=1, source_target_pairs={{0,1},{1,0},{2,3},{3,2},{4,5},{5,4},{6,7},{7,6},{8,9},{9,8},{10,11... | collective-permute-start | bytes 1572872 | tf_op jit(solution)/shard_map/ppermute | solution.py:227
  110.8 13.5 %collective-permute-start.14 = (bf16[256,1024]{1,0:T(8,128)(2,1)S(1)}, bf16[256,1024]{1,0:T(8,128)(2,1)S(1)}, u32[]{:S(2)}, u32[]{:S(2)}) collective-permute-start(bf16[256,1024]{1,0:T(8,128)(2,1)S(1)} %collective-permute-done.7), channel_id=1, source_target_pairs={{0,1},{1,0},{2,3},{3,2},{4,5},{5,4},{6,7},{7,6},{8,9},{9,8},{10,11... | collective-permute-start | bytes 1572872 | tf_op jit(solution)/shard_map/ppermute | solution.py:227
